TPU v7x, 32 devices: a whole 2x2x4 slice. The times are simulated.
32 devices in a mesh: ifg: 16 (over z, y, x), tile: 2 (over core).
Axes of the slice: x: 2, y: 2, z: 4, core: 2. Of those that a mesh axis runs over, the one named last changes fastest.
Arguments:
- phases: float32 [1024, 128, 64], P('ifg', 'tile'), may hold values from -6 to 6
- pairs: int32 [1024, 2], replicated, may hold values from 0 to 299, as said below
- class_weights: float32 [8, 1024], replicated, may hold values from 0.05 to 1
- classes: int32 [128, 64], P('tile', 'ifg'), may hold values from 0 to 7
Outputs:
- corrected: float32 [128, 64, 300], P('tile', 'ifg')
Inputs may be any that keep to these rules, and one draw needn't show every extreme that they name: pairs[i,0] < pairs[i,1] <= pairs[i,0] + 8; some interferogram starts at date 0 and some ends at date 300 - 1.
All inputs are finite; a program needn't handle non-finite values.
Results may differ from a plain program's by a relative error of at most 0.0003.
Values sent between devices are 32-bit elements; how exact they have to be, the bound alone decides.
A program may use at most 128 MiB of HBM per device.

v0:
```python
import jax
import jax.numpy as jnp
from jax import lax
from jax.sharding import PartitionSpec as P

DATES = 300
CLASSES = 8
MAXGAP = 8
R = 3
smooth_weight = 1.0
anchor_weight = 0.1


def with_halo(cells, sides, width):
    for axis, dim in sides:
        count = lax.axis_size(axis)
        ends = count - 1
        head = lax.slice_in_dim(cells, 0, width, axis=dim)
        tail = lax.slice_in_dim(cells, cells.shape[dim] - width, cells.shape[dim], axis=dim)
        cells = jnp.concatenate(
            [
                lax.ppermute(tail, axis, [(i, (i + 1) % count) for i in range(ends)]),
                cells,
                lax.ppermute(head, axis, [((i + 1) % count, i) for i in range(ends)]),
            ],
            axis=dim,
        )
    return cells


def incidence_matrix(pairs):
    dates = jnp.arange(DATES, dtype=jnp.int32)[:, None]
    plus = (dates == pairs[:, 1][None, :]).astype(jnp.float32)
    minus = (dates == pairs[:, 0][None, :]).astype(jnp.float32)
    return (plus, minus)


def prior_matrix():
    second = jnp.arange(DATES - 2, dtype=jnp.int32)[:, None]
    columns = jnp.arange(DATES, dtype=jnp.int32)[None, :]
    diffs = (
        (columns == second).astype(jnp.float32)
        - 2.0 * (columns == second + 1).astype(jnp.float32)
        + (columns == second + 2).astype(jnp.float32)
    )
    curvature = jnp.dot(
        diffs.T, diffs, precision=lax.Precision.HIGHEST, preferred_element_type=jnp.float32
    )
    return smooth_weight * curvature + anchor_weight * jnp.eye(DATES, dtype=jnp.float32)


def class_systems(pairs, plus, minus, weights):
    diagonal = jnp.dot(
        weights,
        (plus + minus).T,
        precision=lax.Precision.HIGHEST,
        preferred_element_type=jnp.float32,
    )
    spacing = pairs[:, 1] - pairs[:, 0]
    offsets = jnp.arange(1, MAXGAP + 1, dtype=jnp.int32)[:, None]
    gap_onehot = (spacing[None, :] == offsets).astype(jnp.float32)
    spread = weights[:, None, :] * gap_onehot[None, :, :]
    band = jnp.einsum("kgi,ai->kga", spread, minus, precision=lax.Precision.HIGHEST)
    row_ids = jnp.arange(DATES, dtype=jnp.int32)[:, None]
    col_ids = jnp.arange(DATES, dtype=jnp.int32)[None, :]
    normal = diagonal[:, :, None] * (row_ids == col_ids).astype(jnp.float32)[None]
    for offset in range(MAXGAP):
        select = (col_ids == row_ids + offset + 1).astype(jnp.float32)
        normal = (
            normal
            - band[:, offset, :, None] * select[None]
            - band[:, offset, None, :] * select.T[None]
        )
    return normal


def invert(matrix):
    factor = jnp.linalg.cholesky(matrix)
    return jax.scipy.linalg.cho_solve((factor, True), jnp.eye(DATES, dtype=jnp.float32))


def filter_taps():
    offsets = jnp.arange(-R, R + 1).astype(jnp.float32)
    values = jnp.exp(-offsets * offsets / 4.5)
    return values / jnp.sum(values)


def pass_columns(padded, filter_weights, width):
    result = filter_weights[0] * padded[:, 0:width]
    for offset in range(1, 2 * R + 1):
        result = result + filter_weights[offset] * padded[:, offset : offset + width]
    return result


def pass_rows(padded, filter_weights, height):
    result = filter_weights[0] * padded[0:height]
    for offset in range(1, 2 * R + 1):
        result = result + filter_weights[offset] * padded[offset : offset + height]
    return result


def date_terms(received, incidence, weight_rows, onehot):
    flat = received.reshape(received.shape[0], -1)
    pixel_weights = jnp.dot(
        weight_rows, onehot, precision=lax.Precision.HIGHEST, preferred_element_type=jnp.float32
    )
    return jnp.einsum("ip,di->pd", pixel_weights * flat, incidence, precision=lax.Precision.HIGHEST)


def on_device(phases, pairs, class_weights, classes):
    plus, minus = incidence_matrix(pairs)
    incidence = plus - minus
    class_share = CLASSES // lax.axis_size("tile")
    first_class = lax.axis_index("tile") * class_share
    own_weights = lax.dynamic_slice_in_dim(class_weights, first_class, class_share, 0)
    own_normal = class_systems(pairs, plus, minus, own_weights)
    own_inverse = jax.vmap(invert)(own_normal + prior_matrix()[None])
    inverse = lax.all_gather(own_inverse, "tile", axis=0, tiled=True)
    tile_rows = phases.shape[1]
    tile_cols = classes.shape[1]
    class_flat = classes.reshape(-1)
    onehot = (class_flat[None, :] == jnp.arange(CLASSES, dtype=jnp.int32)[:, None]).astype(
        jnp.float32
    )
    weight_rows = class_weights.T
    regrouped = lax.all_to_all(phases, "ifg", split_axis=2, concat_axis=0, tiled=True)
    right_terms = date_terms(regrouped, incidence, weight_rows, onehot)
    solution = jnp.zeros((tile_rows * tile_cols, DATES), jnp.float32)
    for member in range(CLASSES):
        solved = jnp.einsum(
            "pd,ed->pe", right_terms, inverse[member], precision=lax.Precision.HIGHEST
        )
        solution = solution + onehot[member][:, None] * solved
    displacement = solution.reshape(tile_rows, tile_cols, DATES)
    filter_weights = filter_taps()
    padded = with_halo(displacement, (("ifg", 1), ("tile", 0)), R)
    across = pass_columns(padded, filter_weights, tile_cols)
    atmosphere = pass_rows(across, filter_weights, tile_rows)
    return displacement - atmosphere


def solution(mesh):
    return jax.shard_map(
        on_device,
        mesh=mesh,
        in_specs=(P("ifg", "tile", None), P(), P(), P("tile", "ifg")),
        out_specs=P("tile", "ifg", None),
        check_vma=False,
    )
```

profile of v0, /device:TPU:13, one launch (start us, length us, event | category | flops | bytes accessed | tf_op | source)
XLA Modules:
  0.0 464.6 jit_solution(6404731645494615155)
XLA Ops:
  7.3 1.3 fusion.6
  9.5 1.4 bitcast_add_fusion
  12.6 4.8 %fusion.2 = f32[4,300,300]{2,1,0:T(8,128)S(1)} fusion(f32[300,300]{1,0:T(8,128)S(1)} %copy.75, f32[300,300]{1,0:T(8,128)S(1)} %copy.74, f32[4,300]{1,0:T(4,128)S(1)} %fusion.6, f32[300,300]{1,0:T(8,128)S(1)} %copy.73, f32[300,300]{1,0:T(8,128)S(1)} %get-tuple-element.96, f32[4,300]{1,0:T(4,128)S(1)} %get-tuple-element.82, ...), kind=kLoop, calls=%fused_computation.36 | loop fusion | flops 19440000 | bytes 8683200 | tf_op jit(solution)/shard_map/vmap(jit(cholesky))/div | solution.py:78
  17.4 1.3 copy-done.2
  18.7 46.9 %custom-call.29 = f32[4,128,128]{2,1,0:T(8,128)S(1)} custom-call(f32[4,128,128]{2,1,0:T(8,128)S(1)} %cholesky.205), custom_call_target="Cholesky" | custom-call | tf_op jit(solution)/shard_map/vmap(jit(cholesky))/cholesky | solution.py:78
  65.8 39.9 %custom-call.30 = f32[4,1,128,128]{2,3,1,0:T(8,128)} custom-call(f32[4,1,128,128]{3,2,1,0:T(8,128)S(1)} %select_bitcast_fusion.1), custom_call_target="InvertDiagBlocksLowerTriangular" | custom-call | tf_op jit(solution)/shard_map/vmap(jit(cholesky))/cholesky | solution.py:78
  105.7 1.5 constant_dynamic-update-slice_fusion.2
  107.2 1.7 convolution_subtract_fusion.3
  109.6 48.5 %custom-call.31 = f32[4,128,128]{2,1,0:T(8,128)} custom-call(f32[4,128,128]{2,1,0:T(8,128)} %cholesky.209), custom_call_target="Cholesky" | custom-call | tf_op jit(solution)/shard_map/vmap(jit(cholesky))/cholesky | solution.py:78
  158.1 1.7 select_reduce_fusion
  159.8 40.1 %custom-call.32 = f32[4,1,128,128]{2,3,1,0:T(8,128)S(1)} custom-call(f32[4,1,128,128]{3,2,1,0:T(8,128)} %get-tuple-element.31), custom_call_target="InvertDiagBlocksLowerTriangular" | custom-call | tf_op jit(solution)/shard_map/vmap(jit(cholesky))/cholesky | solution.py:78
  200.3 1.2 convolution_subtract_fusion.4
  201.5 16.1 %custom-call.33 = f32[4,44,44]{2,1,0:T(8,128)S(1)} custom-call(f32[4,44,44]{2,1,0:T(8,128)S(1)} %convolution_subtract_fusion.4), custom_call_target="Cholesky" | custom-call | tf_op jit(solution)/shard_map/vmap(jit(cholesky))/cholesky | solution.py:78
  218.9 1.8 select_select_fusion
  220.8 4.1 while.1
  221.4 1.4 bitcast_dynamic-update-slice_fusion.2
  223.5 1.4 bitcast_dynamic-update-slice_fusion.2
  225.1 118.7 %custom-call.34 = f32[4,3,128,128]{2,3,1,0:T(8,128)} custom-call(f32[4,3,128,128]{3,2,1,0:T(8,128)S(1)} %pad_maximum_fusion.2), custom_call_target="InvertDiagBlocksLowerTriangular" | custom-call | tf_op jit(solution)/shard_map/vmap(jit(_cho_solve))/triangular_solve | solution.py:79
  343.9 1.6 fusion.72
  346.2 1.6 fusion.81
  348.0 1.3 fusion.24
  349.2 1.3 fusion.92
  350.6 1.3 fusion.91
  351.9 2.0 convolution_subtract_fusion.1
  354.2 1.8 fusion.80
  356.0 1.2 convolution_subtract_fusion.2
  357.2 1.6 fusion.79
  359.0 1.8 copy.89
  360.8 3.1 copy.69
  363.9 2.3 reshape.539
  366.2 6.9 %all-to-all-start = ((f32[16,1,16384]{2,1,0:T(1,128)}), f32[16,1,16384]{2,1,0:T(1,128)S(1)}, u32[]{:S(2)}, u32[]{:S(2)}) async-start(f32[16,1,16384]{2,1,0:T(1,128)} %reshape.539), calls=%async_computation | async-start | bytes 2097152 | tf_op jit(solution)/shard_map/all_to_all | solution.py:126
  373.4 24.5 %all-to-all-done = f32[16,1,16384]{2,1,0:T(1,128)S(1)} async-done(((f32[16,1,16384]{2,1,0:T(1,128)}), f32[16,1,16384]{2,1,0:T(1,128)S(1)}, u32[]{:S(2)}, u32[]{:S(2)}) %all-to-all-start) | async-done | bytes 1048608 | tf_op jit(solution)/shard_map/all_to_all | solution.py:126
  398.4 3.1 reduce.18
  402.4 2.7 copy.70
  405.1 2.0 reshape.515
  407.8 1.4 fusion.5
  409.2 1.8 convolution_multiply_fusion.6
  411.0 1.7 convolution_multiply_fusion.5
  412.7 1.7 convolution_multiply_fusion.4
  414.4 1.7 convolution_multiply_fusion.3
  419.3 2.1 collective-permute-start
  421.5 4.1 collective-permute-start.1
  426.8 4.2 collective-permute-done
  431.0 10.1 %collective-permute-done.1 = f32[64,3,300]{2,1,0:T(4,128)S(1)} collective-permute-done((f32[64,3,300]{2,1,0:T(4,128)S(1)}, f32[64,3,300]{2,1,0:T(4,128)S(1)}, u32[]{:S(2)}, u32[]{:S(2)}) %collective-permute-start.1) | collective-permute-done | bytes 230432 | tf_op jit(solution)/shard_map/ppermute | solution.py:24
  441.1 1.3 collective-permute-start.2
  442.4 3.0 collective-permute-start.3
  446.8 5.0 %fusion.56 = f32[70,4,300]{2,1,0:T(4,128)S(1)} fusion(f32[70,10,300]{2,1,0:T(8,128)S(1)} %pad_maximum_fusion.1, f32[]{:T(128)} %bitcast.39, f32[]{:T(128)} %bitcast.38, f32[]{:T(128)} %bitcast.37, f32[]{:T(128)} %bitcast.36, f32[]{:T(128)} %bitcast.35, f32[]{:T(128)} %bitcast.34, f32[]{:T(128)} %bitcast.33), kind=kLoop, calls=%fused_computation.143 | loop fusion | flops 1092000 | bytes 2688028 | tf_op jit(solution)/shard_map/add | solution.py:91
  451.8 5.5 %fusion.63 = f32[64,4,300]{2,1,0:T(4,128)} fusion(f32[64,4,300]{2,1,0:T(4,128)S(1)} %reshape.516, f32[70,4,300]{2,1,0:T(4,128)S(1)} %fusion.56, f32[]{:T(128)} %bitcast.39, f32[]{:T(128)} %bitcast.38, f32[]{:T(128)} %bitcast.37, f32[]{:T(128)} %bitcast.36, f32[]{:T(128)} %bitcast.35, f32[]{:T(128)} %bitcast.34, f32[]{:T(128)} %bitcast.33), kind=kLoop, calls=%fused_computation.157 | loop fusion | flops 1075200 | bytes 2764828 | tf_op jit(solution)/shard_map/sub | solution.py:139
  (102 shorter events, 16.3 us)
Async XLA Ops:
  6.5 0.8 copy-start
  6.5 0.7 copy-start.5
  6.5 402.6 %all-gather.2.cloned.1.call-start = ((), (), s32[]{:S(2)}) async-start(), calls=%async_computation.1 | async-start | bytes 5603328 | tf_op jit(solution)/shard_map/all_gather | solution.py:118
  6.7 2.7 copy-start.3
  17.4 1.3 copy-start.2
  217.7 1.3 copy-start.1
  343.9 4.0 slice-start
  363.9 9.3 %copy-start.6 = (s32[64,4]{0,1:T(4,128)S(1)}, s32[64,4]{0,1:T(4,128)}, u32[]{:S(2)}) copy-start(s32[64,4]{0,1:T(4,128)} %param.7) | copy-start | bytes 3076
  366.2 31.7 %all-to-all-start = ((f32[16,1,16384]{2,1,0:T(1,128)}), f32[16,1,16384]{2,1,0:T(1,128)S(1)}, u32[]{:S(2)}, u32[]{:S(2)}) async-start(f32[16,1,16384]{2,1,0:T(1,128)} %reshape.539), calls=%async_computation | async-start | bytes 2097152 | tf_op jit(solution)/shard_map/all_to_all | solution.py:126
  409.2 6.9 %copy-start.4 = (f32[8,300,300]{2,1,0:T(8,128)S(1)}, f32[8,300,300]{2,1,0:T(8,128)}, u32[]{:S(2)}) copy-start(f32[8,300,300]{2,1,0:T(8,128)} %all-gather.2.cloned.1.call-done) | copy-start | bytes 8640004
  419.3 11.7 %collective-permute-start = (f32[64,3,300]{2,1,0:T(4,128)S(1)}, f32[64,3,300]{2,1,0:T(4,128)S(1)}, u32[]{:S(2)}, u32[]{:S(2)}) collective-permute-start(f32[64,3,300]{2,1,0:T(4,128)S(1)} %get-tuple-element.29), channel_id=1, source_target_pairs={{0,2},{2,4},{4,6},{6,8},{8,10},{10,12},{12,14},{14,16},{16,18},{18... | collective-permute-start | bytes 691208 | tf_op jit(solution)/shard_map/ppermute | solution.py:22
  421.5 19.6 %collective-permute-start.1 = (f32[64,3,300]{2,1,0:T(4,128)S(1)}, f32[64,3,300]{2,1,0:T(4,128)S(1)}, u32[]{:S(2)}, u32[]{:S(2)}) collective-permute-start(f32[64,3,300]{2,1,0:T(4,128)S(1)} %get-tuple-element.30), channel_id=1, source_target_pairs={{2,0},{4,2},{6,4},{8,6},{10,8},{12,10},{14,12},{16,14},{18,16},{20... | collective-permute-start | bytes 691208 | tf_op jit(solution)/shard_map/ppermute | solution.py:24
  441.1 5.0 %collective-permute-start.2 = (f32[3,10,300]{2,1,0:T(8,128)S(1)}, f32[3,10,300]{2,1,0:T(8,128)S(1)}, u32[]{:S(2)}, u32[]{:S(2)}) collective-permute-start(f32[3,10,300]{2,1,0:T(8,128)S(1)} %get-tuple-element.25), channel_id=1, source_target_pairs={{0,1},{2,3},{4,5},{6,7},{8,9},{10,11},{12,13},{14,15},{16,17},{18,... | collective-permute-start | bytes 108008 | tf_op jit(solution)/shard_map/ppermute | solution.py:22
  442.4 3.9 collective-permute-start.3
Sparse Core Ops, SparseCore 0:
  360.9 14.8 all-gather.1
where the time goes:
time: 470 us; the launch traced here: 465 us
  other arithmetic  336 us (71%)
  waiting for transfers between devices  39 us (8%)
  matrix products  34.2 us (7%)
  local copies, waits for them, and re-layouts  23.4 us (5%)
  starting transfers between devices  17.5 us (4%)
  between operations  14.6 us (3%)
    another operation x14, other arithmetic, invert(): factor = jnp.linalg.cholesky(matrix)  194 us
    another operation x9, other arithmetic, invert(): jax.scipy.linalg.cho_solve((factor, True), jnp.eye(DATES, dtype=jnp.float...  121 us
    all_to_all x1, waiting for transfers between devices, on_device(): lax.all_to_all(phases, 'ifg', split_axis=2, concat_axis=0, tiled=True)  24.5 us
    another operation x10, matrix products, invert(): jax.scipy.linalg.cho_solve((factor, True), jnp.eye(DATES, dtype=jnp.float...  14.5 us
    ppermute x2, waiting for transfers between devices, with_halo(): lax.ppermute(head, axis, [((i + 1) % count, i) for i in range(ends)])  10.3 us
    dot_general x8, matrix products, on_device(): jnp.einsum('pd,ed->pe', right_terms, inverse[member], precision=lax.Preci...  9.61 us
  transfers between devices with their start and end apart: 6, of which 4 were waited for; matrix products, arithmetic and copies ran while one was open for 4% of the time, Pallas kernels for 0%

commit v1 on v0

--- a/solution.py
+++ b/solution.py
@@ -123,7 +123,15 @@
         jnp.float32
     )
     weight_rows = class_weights.T
-    regrouped = lax.all_to_all(phases, "ifg", split_axis=2, concat_axis=0, tiled=True)
+    ways, here = (lax.axis_size("ifg"), lax.axis_index("ifg"))
+    width_2 = phases.shape[2] // ways
+    turned = jnp.roll(phases, -here * width_2, axis=2)
+    got = [lax.slice_in_dim(turned, 0, width_2, axis=2)]
+    for far in range(1, ways):
+        sent = lax.slice_in_dim(turned, far * width_2, (far + 1) * width_2, axis=2)
+        got.append(lax.ppermute(sent, "ifg", [(d, (d + far) % ways) for d in range(ways)]))
+    line = jnp.concatenate(got[::-1], axis=0)
+    regrouped = jnp.roll(line, (here + 1) * got[0].shape[0], axis=0)
     right_terms = date_terms(regrouped, incidence, weight_rows, onehot)
     solution = jnp.zeros((tile_rows * tile_cols, DATES), jnp.float32)
     for member in range(CLASSES):

time: 470 us -> 502 us (1.068)
  starting transfers between devices: 17.5 us -> 51.7 us
  waiting for transfers between devices: 39 us -> 22.4 us
  local copies, waits for them, and re-layouts: 23.4 us -> 37.8 us
    ppermute x0 -> x15, starting transfers between devices: none -> 39.6 us  [on_device(): lax.ppermute(sent, 'ifg', [(d, (d + far) % ways) for d in range(ways)])]
    all_to_all x1 -> x0, waiting for transfers between devices: 24.5 us -> none  [on_device(): lax.all_to_all(phases, 'ifg', split_axis=2, concat_axis=0, tiled=True)]
    ppermute x0 -> x15, local copies, waits for them, and re-layouts: none -> 15.2 us  [on_device(): lax.ppermute(sent, 'ifg', [(d, (d + far) % ways) for d in range(ways)])]
    ppermute x0 -> x15, waiting for transfers between devices: none -> 8.11 us  [on_device(): lax.ppermute(sent, 'ifg', [(d, (d + far) % ways) for d in range(ways)])]
    all_to_all x1 -> x0, starting transfers between devices: 6.95 us -> none  [on_device(): lax.all_to_all(phases, 'ifg', split_axis=2, concat_axis=0, tiled=True)]
  transfers between devices with their start and end apart: 6 -> 20, of which waited for: 4 -> 6; matrix products, arithmetic and copies ran while one was open for 4% -> 6% of each run, Pallas kernels for 0% -> 0%
where the time goes in v1:
time: 502 us; the launch traced here: 494 us
  other arithmetic  334 us (67%)
  starting transfers between devices  51.7 us (10%)
  local copies, waits for them, and re-layouts  37.8 us (8%)
  matrix products  34.3 us (7%)
  waiting for transfers between devices  22.4 us (4%)
  between operations  14.4 us (3%)
    another operation x14, other arithmetic, invert(): factor = jnp.linalg.cholesky(matrix)  194 us
    another operation x9, other arithmetic, invert(): jax.scipy.linalg.cho_solve((factor, True), jnp.eye(DATES, dtype=jnp.float...  121 us
    ppermute x15, starting transfers between devices, on_device(): lax.ppermute(sent, 'ifg', [(d, (d + far) % ways) for d in range(ways)])  39.6 us
    ppermute x15, local copies, waits for them, and re-layouts, on_device(): lax.ppermute(sent, 'ifg', [(d, (d + far) % ways) for d in range(ways)])  15.2 us
    another operation x10, matrix products, invert(): jax.scipy.linalg.cho_solve((factor, True), jnp.eye(DATES, dtype=jnp.float...  14.5 us
    ppermute x2, waiting for transfers between devices, with_halo(): lax.ppermute(head, axis, [((i + 1) % count, i) for i in range(ends)])  12.7 us
  transfers between devices with their start and end apart: 20, of which 6 were waited for; matrix products, arithmetic and copies ran while one was open for 6% of the time, Pallas kernels for 0%

profile of v1, /device:TPU:13, one launch (start us, length us, event | category | flops | bytes accessed | tf_op | source)
XLA Modules:
  0.0 494.2 jit_solution(11012547785174135596)
XLA Ops:
  9.5 1.4 bitcast_add_fusion
  12.6 4.5 fusion.3
  18.4 46.9 %custom-call.29 = f32[4,128,128]{2,1,0:T(8,128)S(1)} custom-call(f32[4,128,128]{2,1,0:T(8,128)S(1)} %cholesky.205), custom_call_target="Cholesky" | custom-call | tf_op jit(solution)/shard_map/vmap(jit(cholesky))/cholesky | solution.py:78
  65.5 39.9 %custom-call.30 = f32[4,1,128,128]{2,3,1,0:T(8,128)} custom-call(f32[4,1,128,128]{3,2,1,0:T(8,128)S(1)} %select_bitcast_fusion.1), custom_call_target="InvertDiagBlocksLowerTriangular" | custom-call | tf_op jit(solution)/shard_map/vmap(jit(cholesky))/cholesky | solution.py:78
  105.4 1.5 constant_dynamic-update-slice_fusion.2
  106.9 1.7 convolution_subtract_fusion.3
  109.3 48.5 %custom-call.31 = f32[4,128,128]{2,1,0:T(8,128)} custom-call(f32[4,128,128]{2,1,0:T(8,128)} %cholesky.209), custom_call_target="Cholesky" | custom-call | tf_op jit(solution)/shard_map/vmap(jit(cholesky))/cholesky | solution.py:78
  157.9 1.7 select_reduce_fusion
  159.6 40.1 %custom-call.32 = f32[4,1,128,128]{2,3,1,0:T(8,128)S(1)} custom-call(f32[4,1,128,128]{3,2,1,0:T(8,128)} %get-tuple-element.47), custom_call_target="InvertDiagBlocksLowerTriangular" | custom-call | tf_op jit(solution)/shard_map/vmap(jit(cholesky))/cholesky | solution.py:78
  201.2 16.1 %custom-call.33 = f32[4,44,44]{2,1,0:T(8,128)S(1)} custom-call(f32[4,44,44]{2,1,0:T(8,128)S(1)} %convolution_subtract_fusion.4), custom_call_target="Cholesky" | custom-call | tf_op jit(solution)/shard_map/vmap(jit(cholesky))/cholesky | solution.py:78
  218.7 1.8 select_select_fusion
  220.5 3.9 while.1
  224.7 118.9 %custom-call.34 = f32[4,3,128,128]{2,3,1,0:T(8,128)} custom-call(f32[4,3,128,128]{3,2,1,0:T(8,128)S(1)} %pad_maximum_fusion.2), custom_call_target="InvertDiagBlocksLowerTriangular" | custom-call | tf_op jit(solution)/shard_map/vmap(jit(_cho_solve))/triangular_solve | solution.py:79
  343.7 1.6 fusion.73
  346.0 1.6 fusion.82
  351.7 2.0 convolution_subtract_fusion.1
  354.0 1.8 fusion.81
  357.0 1.6 fusion.80
  358.8 1.8 copy.154
  360.7 3.1 copy.101
  367.2 3.3 collective-permute-start.3
  370.5 2.1 collective-permute-start.4
  374.1 3.4 collective-permute-start.6
  377.5 2.0 collective-permute-start.7
  379.5 3.0 collective-permute-start.8
  382.5 2.1 collective-permute-start.9
  384.6 1.7 collective-permute-done.5
  387.2 5.9 %collective-permute-done.6 = f32[64,64,4]{1,0,2:T(8,128)S(1)} collective-permute-done((f32[64,64,4]{1,0,2:T(8,128)S(1)}, f32[64,64,4]{1,0,2:T(8,128)S(1)}, u32[]{:S(2)}, u32[]{:S(2)}) %collective-permute-start.6) | collective-permute-done | bytes 65568 | tf_op jit(solution)/shard_map/ppermute | solution.py:132
  393.1 8.2 %collective-permute-start.11 = (f32[64,64,4]{1,0,2:T(8,128)S(1)}, f32[64,64,4]{1,0,2:T(8,128)S(1)}, u32[]{:S(2)}, u32[]{:S(2)}) collective-permute-start(f32[64,64,4]{1,0,2:T(8,128)S(1)} %get-tuple-element.29), channel_id=1, source_target_pairs={{0,8},{2,10},{4,12},{6,14},{8,16},{10,18},{12,20},{14,22},{16,24},... | collective-permute-start | bytes 196616 | tf_op jit(solution)/shard_map/ppermute | solution.py:132
  401.4 11.6 %collective-permute-start.12 = (f32[64,64,4]{1,0,2:T(8,128)S(1)}, f32[64,64,4]{1,0,2:T(8,128)S(1)}, u32[]{:S(2)}, u32[]{:S(2)}) collective-permute-start(f32[64,64,4]{1,0,2:T(8,128)S(1)} %get-tuple-element.28), channel_id=1, source_target_pairs={{0,6},{2,8},{4,10},{6,12},{8,14},{10,16},{12,18},{14,20},{16,22},{... | collective-permute-start | bytes 196616 | tf_op jit(solution)/shard_map/ppermute | solution.py:132
  414.7 1.7 copy.104
  416.3 1.7 copy.105
  418.0 1.7 copy.106
  419.6 1.7 copy.107
  428.8 3.8 concatenate.43
  433.0 1.7 copy.135
  434.7 1.6 reshape.514
  437.7 1.8 convolution_multiply_fusion.6
  439.6 1.7 convolution_multiply_fusion.5
  441.3 1.7 convolution_multiply_fusion.4
  443.0 1.7 convolution_multiply_fusion.3
  447.9 5.8 %collective-permute-start.15 = (f32[64,3,300]{2,1,0:T(4,128)S(1)}, f32[64,3,300]{2,1,0:T(4,128)S(1)}, u32[]{:S(2)}, u32[]{:S(2)}) collective-permute-start(f32[64,3,300]{2,1,0:T(4,128)S(1)} %get-tuple-element.45), channel_id=1, source_target_pairs={{0,2},{2,4},{4,6},{6,8},{8,10},{10,12},{12,14},{14,16},{16,18},{18... | collective-permute-start | bytes 691208 | tf_op jit(solution)/shard_map/ppermute | solution.py:22
  453.7 1.9 collective-permute-start.16
  456.9 1.5 collective-permute-done.15
  458.4 12.5 %collective-permute-done.16 = f32[64,3,300]{2,1,0:T(4,128)S(1)} collective-permute-done((f32[64,3,300]{2,1,0:T(4,128)S(1)}, f32[64,3,300]{2,1,0:T(4,128)S(1)}, u32[]{:S(2)}, u32[]{:S(2)}) %collective-permute-start.16) | collective-permute-done | bytes 230432 | tf_op jit(solution)/shard_map/ppermute | solution.py:24
  472.3 3.0 collective-permute-start.18
  476.6 5.1 %fusion.57 = f32[70,4,300]{2,1,0:T(4,128)S(1)} fusion(f32[70,10,300]{2,1,0:T(8,128)S(1)} %pad_maximum_fusion.1, f32[]{:T(128)} %bitcast.37, f32[]{:T(128)} %bitcast.36, f32[]{:T(128)} %bitcast.35, f32[]{:T(128)} %bitcast.34, f32[]{:T(128)} %bitcast.33, f32[]{:T(128)} %bitcast.32, f32[]{:T(128)} %bitcast.31), kind=kLoop, calls=%fused_computation.146 | loop fusion | flops 1092000 | bytes 2688028 | tf_op jit(solution)/shard_map/add | solution.py:91
  481.7 5.5 %fusion.64 = f32[64,4,300]{2,1,0:T(4,128)} fusion(f32[64,4,300]{2,1,0:T(4,128)S(1)} %reshape.515, f32[70,4,300]{2,1,0:T(4,128)S(1)} %fusion.57, f32[]{:T(128)} %bitcast.37, f32[]{:T(128)} %bitcast.36, f32[]{:T(128)} %bitcast.35, f32[]{:T(128)} %bitcast.34, f32[]{:T(128)} %bitcast.33, f32[]{:T(128)} %bitcast.32, f32[]{:T(128)} %bitcast.31), kind=kLoop, calls=%fused_computation.160 | loop fusion | flops 1075200 | bytes 2764828 | tf_op jit(solution)/shard_map/sub | solution.py:147
  (150 shorter events, 43.5 us)
Async XLA Ops:
  6.5 0.8 copy-start
  6.5 0.7 copy-start.7
  6.5 431.2 %all-gather.2.cloned.1.call-start = ((), (), s32[]{:S(2)}) async-start(), calls=%async_computation | async-start | bytes 5603328 | tf_op jit(solution)/shard_map/all_gather | solution.py:118
  6.7 2.7 copy-start.3
  17.1 1.3 copy-start.2
  217.4 1.3 copy-start.1
  343.7 4.0 slice-start
  364.7 8.0 %copy-start.8 = (s32[64,4]{0,1:T(4,128)S(1)}, s32[64,4]{0,1:T(4,128)}, u32[]{:S(2)}) copy-start(s32[64,4]{0,1:T(4,128)} %param.7) | copy-start | bytes 3076
  364.9 8.6 %collective-permute-start = (f32[64,64,4]{1,0,2:T(8,128)S(1)}, f32[64,64,4]{1,0,2:T(8,128)S(1)}, u32[]{:S(2)}, u32[]{:S(2)}) collective-permute-start(f32[64,64,4]{1,0,2:T(8,128)S(1)} %get-tuple-element.40), channel_id=1, source_target_pairs={{0,30},{2,0},{4,2},{6,4},{8,6},{10,8},{12,10},{14,12},{16,14},{18,... | collective-permute-start | bytes 196616 | tf_op jit(solution)/shard_map/ppermute | solution.py:132
  366.1 8.0 %collective-permute-start.1 = (f32[64,64,4]{1,0,2:T(8,128)S(1)}, f32[64,64,4]{1,0,2:T(8,128)S(1)}, u32[]{:S(2)}, u32[]{:S(2)}) collective-permute-start(f32[64,64,4]{1,0,2:T(8,128)S(1)} %get-tuple-element.39), channel_id=1, source_target_pairs={{0,28},{2,30},{4,0},{6,2},{8,4},{10,6},{12,8},{14,10},{16,12},{18,... | collective-permute-start | bytes 196616 | tf_op jit(solution)/shard_map/ppermute | solution.py:132
  367.2 10.3 %collective-permute-start.2 = (f32[64,64,4]{1,0,2:T(8,128)S(1)}, f32[64,64,4]{1,0,2:T(8,128)}, u32[]{:S(2)}, u32[]{:S(2)}) collective-permute-start(f32[64,64,4]{1,0,2:T(8,128)S(1)} %get-tuple-element.38), channel_id=1, source_target_pairs={{0,26},{2,28},{4,30},{6,0},{8,2},{10,4},{12,6},{14,8},{16,10},{18,... | collective-permute-start | bytes 196616 | tf_op jit(solution)/shard_map/ppermute | solution.py:132
  367.2 12.3 %collective-permute-start.3 = (f32[64,64,4]{1,0,2:T(8,128)S(1)}, f32[64,64,4]{1,0,2:T(8,128)}, u32[]{:S(2)}, u32[]{:S(2)}) collective-permute-start(f32[64,64,4]{1,0,2:T(8,128)S(1)} %get-tuple-element.37), channel_id=1, source_target_pairs={{0,24},{2,26},{4,28},{6,30},{8,0},{10,2},{12,4},{14,6},{16,8},{18,... | collective-permute-start | bytes 196616 | tf_op jit(solution)/shard_map/ppermute | solution.py:132
  370.5 11.9 %collective-permute-start.4 = (f32[64,64,4]{1,0,2:T(8,128)S(1)}, f32[64,64,4]{1,0,2:T(8,128)}, u32[]{:S(2)}, u32[]{:S(2)}) collective-permute-start(f32[64,64,4]{1,0,2:T(8,128)S(1)} %get-tuple-element.36), channel_id=1, source_target_pairs={{0,22},{2,24},{4,26},{6,28},{8,30},{10,0},{12,2},{14,4},{16,6},{18... | collective-permute-start | bytes 196616 | tf_op jit(solution)/shard_map/ppermute | solution.py:132
  373.5 40.0 %copy-start.5 = (f32[64,64,4]{1,0,2:T(8,128)}, f32[64,64,4]{1,0,2:T(8,128)S(1)}, u32[]{:S(2)}) copy-start(f32[64,64,4]{1,0,2:T(8,128)S(1)} %collective-permute-done) | copy-start | bytes 196612
  373.5 12.8 %collective-permute-start.5 = (f32[64,64,4]{1,0,2:T(8,128)S(1)}, f32[64,64,4]{1,0,2:T(8,128)S(1)}, u32[]{:S(2)}, u32[]{:S(2)}) collective-permute-start(f32[64,64,4]{1,0,2:T(8,128)S(1)} %get-tuple-element.35), channel_id=1, source_target_pairs={{0,20},{2,22},{4,24},{6,26},{8,28},{10,30},{12,0},{14,2},{16,4},{1... | collective-permute-start | bytes 196616 | tf_op jit(solution)/shard_map/ppermute | solution.py:132
  374.1 39.6 %copy-start.6 = (f32[64,64,4]{1,0,2:T(8,128)}, f32[64,64,4]{1,0,2:T(8,128)S(1)}, u32[]{:S(2)}) copy-start(f32[64,64,4]{1,0,2:T(8,128)S(1)} %collective-permute-done.1) | copy-start | bytes 196612
  374.1 19.1 %collective-permute-start.6 = (f32[64,64,4]{1,0,2:T(8,128)S(1)}, f32[64,64,4]{1,0,2:T(8,128)S(1)}, u32[]{:S(2)}, u32[]{:S(2)}) collective-permute-start(f32[64,64,4]{1,0,2:T(8,128)S(1)} %get-tuple-element.34), channel_id=1, source_target_pairs={{0,18},{2,20},{4,22},{6,24},{8,26},{10,28},{12,30},{14,0},{16,2},{... | collective-permute-start | bytes 196616 | tf_op jit(solution)/shard_map/ppermute | solution.py:132
  377.5 23.9 %collective-permute-start.7 = (f32[64,64,4]{1,0,2:T(8,128)S(1)}, f32[64,64,4]{1,0,2:T(8,128)S(1)}, u32[]{:S(2)}, u32[]{:S(2)}) collective-permute-start(f32[64,64,4]{1,0,2:T(8,128)S(1)} %get-tuple-element.33), channel_id=1, source_target_pairs={{0,16},{2,18},{4,20},{6,22},{8,24},{10,26},{12,28},{14,30},{16,0},... | collective-permute-start | bytes 196616 | tf_op jit(solution)/shard_map/ppermute | solution.py:132
  379.5 33.5 %collective-permute-start.8 = (f32[64,64,4]{1,0,2:T(8,128)S(1)}, f32[64,64,4]{1,0,2:T(8,128)S(1)}, u32[]{:S(2)}, u32[]{:S(2)}) collective-permute-start(f32[64,64,4]{1,0,2:T(8,128)S(1)} %get-tuple-element.32), channel_id=1, source_target_pairs={{0,14},{2,16},{4,18},{6,20},{8,22},{10,24},{12,26},{14,28},{16,30}... | collective-permute-start | bytes 196616 | tf_op jit(solution)/shard_map/ppermute | solution.py:132
  382.5 30.5 %collective-permute-start.9 = (f32[64,64,4]{1,0,2:T(8,128)S(1)}, f32[64,64,4]{1,0,2:T(8,128)S(1)}, u32[]{:S(2)}, u32[]{:S(2)}) collective-permute-start(f32[64,64,4]{1,0,2:T(8,128)S(1)} %get-tuple-element.31), channel_id=1, source_target_pairs={{0,12},{2,14},{4,16},{6,18},{8,20},{10,22},{12,24},{14,26},{16,28}... | collective-permute-start | bytes 196616 | tf_op jit(solution)/shard_map/ppermute | solution.py:132
  386.3 38.7 %collective-permute-start.10 = (f32[64,64,4]{1,0,2:T(8,128)S(1)}, f32[64,64,4]{1,0,2:T(8,128)S(1)}, u32[]{:S(2)}, u32[]{:S(2)}) collective-permute-start(f32[64,64,4]{1,0,2:T(8,128)S(1)} %get-tuple-element.30), channel_id=1, source_target_pairs={{0,10},{2,12},{4,14},{6,16},{8,18},{10,20},{12,22},{14,24},{16,26}... | collective-permute-start | bytes 196616 | tf_op jit(solution)/shard_map/ppermute | solution.py:132
  393.1 32.7 %collective-permute-start.11 = (f32[64,64,4]{1,0,2:T(8,128)S(1)}, f32[64,64,4]{1,0,2:T(8,128)S(1)}, u32[]{:S(2)}, u32[]{:S(2)}) collective-permute-start(f32[64,64,4]{1,0,2:T(8,128)S(1)} %get-tuple-element.29), channel_id=1, source_target_pairs={{0,8},{2,10},{4,12},{6,14},{8,16},{10,18},{12,20},{14,22},{16,24},... | collective-permute-start | bytes 196616 | tf_op jit(solution)/shard_map/ppermute | solution.py:132
  401.4 25.2 %collective-permute-start.12 = (f32[64,64,4]{1,0,2:T(8,128)S(1)}, f32[64,64,4]{1,0,2:T(8,128)S(1)}, u32[]{:S(2)}, u32[]{:S(2)}) collective-permute-start(f32[64,64,4]{1,0,2:T(8,128)S(1)} %get-tuple-element.28), channel_id=1, source_target_pairs={{0,6},{2,8},{4,10},{6,12},{8,14},{10,16},{12,18},{14,20},{16,22},{... | collective-permute-start | bytes 196616 | tf_op jit(solution)/shard_map/ppermute | solution.py:132
  413.0 14.3 %collective-permute-start.13 = (f32[64,64,4]{1,0,2:T(8,128)S(1)}, f32[64,64,4]{1,0,2:T(8,128)S(1)}, u32[]{:S(2)}, u32[]{:S(2)}) collective-permute-start(f32[64,64,4]{1,0,2:T(8,128)S(1)} %get-tuple-element.27), channel_id=1, source_target_pairs={{0,4},{2,6},{4,8},{6,10},{8,12},{10,14},{12,16},{14,18},{16,20},{1... | collective-permute-start | bytes 196616 | tf_op jit(solution)/shard_map/ppermute | solution.py:132
  413.0 15.1 %collective-permute-start.14 = (f32[64,64,4]{1,0,2:T(8,128)S(1)}, f32[64,64,4]{1,0,2:T(8,128)S(1)}, u32[]{:S(2)}, u32[]{:S(2)}) collective-permute-start(f32[64,64,4]{1,0,2:T(8,128)S(1)} %get-tuple-element.26), channel_id=1, source_target_pairs={{0,2},{2,4},{4,6},{6,8},{8,10},{10,12},{12,14},{14,16},{16,18},{18... | collective-permute-start | bytes 196616 | tf_op jit(solution)/shard_map/ppermute | solution.py:132
  437.7 7.0 %copy-start.4 = (f32[8,300,300]{2,1,0:T(8,128)S(1)}, f32[8,300,300]{2,1,0:T(8,128)}, u32[]{:S(2)}) copy-start(f32[8,300,300]{2,1,0:T(8,128)} %all-gather.2.cloned.1.call-done) | copy-start | bytes 8640004
  447.9 10.5 %collective-permute-start.15 = (f32[64,3,300]{2,1,0:T(4,128)S(1)}, f32[64,3,300]{2,1,0:T(4,128)S(1)}, u32[]{:S(2)}, u32[]{:S(2)}) collective-permute-start(f32[64,3,300]{2,1,0:T(4,128)S(1)} %get-tuple-element.45), channel_id=1, source_target_pairs={{0,2},{2,4},{4,6},{6,8},{8,10},{10,12},{12,14},{14,16},{16,18},{18... | collective-permute-start | bytes 691208 | tf_op jit(solution)/shard_map/ppermute | solution.py:22
  453.7 17.2 %collective-permute-start.16 = (f32[64,3,300]{2,1,0:T(4,128)S(1)}, f32[64,3,300]{2,1,0:T(4,128)S(1)}, u32[]{:S(2)}, u32[]{:S(2)}) collective-permute-start(f32[64,3,300]{2,1,0:T(4,128)S(1)} %get-tuple-element.46), channel_id=1, source_target_pairs={{2,0},{4,2},{6,4},{8,6},{10,8},{12,10},{14,12},{16,14},{18,16},{20... | collective-permute-start | bytes 691208 | tf_op jit(solution)/shard_map/ppermute | solution.py:24
  471.0 5.0 %collective-permute-start.17 = (f32[3,10,300]{2,1,0:T(8,128)S(1)}, f32[3,10,300]{2,1,0:T(8,128)S(1)}, u32[]{:S(2)}, u32[]{:S(2)}) collective-permute-start(f32[3,10,300]{2,1,0:T(8,128)S(1)} %get-tuple-element.41), channel_id=1, source_target_pairs={{0,1},{2,3},{4,5},{6,7},{8,9},{10,11},{12,13},{14,15},{16,17},{18,... | collective-permute-start | bytes 108008 | tf_op jit(solution)/shard_map/ppermute | solution.py:22
  472.3 3.9 collective-permute-start.18
Sparse Core Ops, SparseCore 0:
  360.8 14.8 all-gather.1
